TPU v7x, 32 devices: a whole 2x2x4 slice. The times are simulated.
32 devices in a mesh: dp: 4 (over x, core), mp: 8 (over z, y).
Axes of the slice: x: 2, y: 2, z: 4, core: 2. Of those that a mesh axis runs over, the one named last changes fastest.
Arguments:
- prompt_rows: bfloat16 [16384, 2048], P(('dp', 'mp')), may hold values from -6 to 6
- step_rows: bfloat16 [16, 2048], P('dp', 'mp'), may hold values from -6 to 6
- attn_gain: float32 [2048], replicated, may hold values from 0.1 to 1.9
- latent_gain: float32 [512], replicated, may hold values from 0.1 to 1.9
- joined_qkva: float32 [2048, 3648], P('dp', 'mp'), may hold values from -2.4748737 to 2.4748737
- kv_up: float32 [512, 4096], P('dp', 'mp'), may hold values from -0.25 to 0.25
- out_proj: float32 [2048, 2048], P('dp', 'mp'), may hold values from -1.5 to 1.5
- latent_cache: bfloat16 [256, 16, 576], P(('dp', 'mp')), may hold values from -6 to 6
- page_table: int32 [16, 8], P('dp'), may hold values from 0 to 63, as said below
- cached_lengths: int32 [16], P('dp'), may hold values from 1 to 127, as said below
Outputs:
- prompt_out: bfloat16 [16384, 2048], P(('dp', 'mp'))
- step_out: bfloat16 [16, 2048], P('dp', 'mp')
Inputs may be any that keep to these rules, and one draw needn't show every extreme that they name: `page_table`: row r lists the slots of r's 8 pages, numbered within the pool of r's index of dp; slot g lies on index g // 8 of mp. No slot is listed twice within one index of dp. `cached_lengths`: some request has 127 cached tokens and some has one.
All inputs are finite; a program needn't handle non-finite values.
Results may differ from a plain program's by a relative error of at most 0.015.
Values may be sent and summed in bfloat16 or wider, within the bound.
A program may use at most 128 MiB of HBM per device.

v0:
```python
import math

import jax
import jax.numpy as jnp
from jax import lax
from jax.sharding import PartitionSpec as P

H = 16
DN = 128
DR = 64
DV = 128
LAT = 512
LEN = 512


NORM_EPS = 1e-06
ROPE_BASE = 50000.0
MASKED = -1e30


def merged(x, axis, combine):
    everything = jax.tree.map(
        lambda part, kind: lax.all_gather(part.astype(kind), axis),
        x,
        jax.tree.map(lambda a: jnp.bfloat16 if a.dtype == jnp.float32 else a.dtype, x),
    )

    def take(k):
        return jax.tree.map(lambda part, own: part[k].astype(own.dtype), everything, x)

    return lax.fori_loop(
        1, lax.axis_size(axis), lambda k, so_far: combine(so_far, take(k)), take(0)
    )


def rms_scale(values, scales):
    widened = values.astype(jnp.float32)
    mean_square = jnp.mean(widened * widened, axis=-1, keepdims=True)
    return widened * lax.rsqrt(mean_square + NORM_EPS) * scales


def rotate(values, positions):
    rot_width = values.shape[-1]
    half_width = rot_width // 2
    freq_steps = jnp.arange(half_width, dtype=jnp.float32)
    inv_freqs = jnp.exp(freq_steps * (-2.0 * math.log(ROPE_BASE) / rot_width))
    angles = positions.astype(jnp.float32)[:, None] * inv_freqs[None, :]
    angle_shape = (positions.shape[0],) + (1,) * (values.ndim - 2) + (half_width,)
    cosine = jnp.cos(angles).reshape(angle_shape)
    sine_part = jnp.sin(angles).reshape(angle_shape)
    lower_half = values[..., :half_width]
    upper_half = values[..., half_width:]
    return jnp.concatenate(
        [
            lower_half * cosine - upper_half * sine_part,
            upper_half * cosine + lower_half * sine_part,
        ],
        axis=-1,
    )


def queries_keys(projected, positions, latent_gain, up_heads):
    head_cols = H * (DN + DR)
    row_count = projected.shape[0]
    query_cols = projected[:, :head_cols].reshape(row_count, H, DN + DR)
    query_rot = rotate(query_cols[..., DN:].astype(jnp.float32), positions).astype(jnp.bfloat16)
    latent = rms_scale(projected[:, head_cols : head_cols + LAT], latent_gain).astype(jnp.bfloat16)
    key_rot = rotate(projected[:, head_cols + LAT :].astype(jnp.float32), positions).astype(
        jnp.bfloat16
    )
    query_lat = jnp.einsum(
        "rhn,lhn->rhl", query_cols[..., :DN], up_heads[..., :DN], preferred_element_type=jnp.float32
    ).astype(jnp.bfloat16)
    queries = jnp.concatenate([query_lat, query_rot], axis=-1)
    key_rows = jnp.concatenate([latent, key_rot], axis=-1)
    return (queries, key_rows)


def prompt_attention(queries, query_ids, all_keys, all_ids, score_scale):
    row_count = queries.shape[0]
    block_rows = min(row_count, 512)
    block_count = row_count // block_rows
    query_blocks = queries.reshape(block_count, block_rows, H, queries.shape[-1])
    id_blocks = query_ids.reshape(block_count, block_rows)
    latent_keys = all_keys[:, :LAT]

    def one_block(block_args):
        query_part, id_part = block_args
        scores = (
            jnp.einsum("qhc,kc->qhk", query_part, all_keys, preferred_element_type=jnp.float32)
            * score_scale
        )
        same_prompt = id_part[:, None] // LEN == all_ids[None, :] // LEN
        allowed = same_prompt & (all_ids[None, :] <= id_part[:, None])
        scores = jnp.where(allowed[:, None, :], scores, MASKED)
        peak_score = jnp.max(scores, axis=-1, keepdims=True)
        weights = jnp.where(allowed[:, None, :], jnp.exp(scores - peak_score), 0.0)
        weight_sum = jnp.sum(weights, axis=-1, keepdims=True)
        summed = jnp.einsum(
            "qhk,kl->qhl",
            weights.astype(jnp.bfloat16),
            latent_keys,
            preferred_element_type=jnp.float32,
        )
        return (summed / weight_sum).astype(jnp.bfloat16)

    return lax.map(one_block, (query_blocks, id_blocks)).reshape(row_count, H, LAT)


def page_attention(queries, latent_cache, page_table, cached_lengths, mp_index, score_scale):
    slot_count = latent_cache.shape[0]
    page_rows = latent_cache.shape[1]
    flat_cache = latent_cache.reshape(slot_count * page_rows, latent_cache.shape[2])
    slot_ids = mp_index * slot_count + jnp.arange(slot_count, dtype=jnp.int32)
    matches = page_table[:, :, None] == slot_ids[None, None, :]
    owned = jnp.any(matches, axis=1)
    page_numbers = jnp.arange(page_table.shape[1], dtype=jnp.int32)[None, :, None]
    page_index = jnp.sum(jnp.where(matches, page_numbers, 0), axis=1)
    key_position = (
        page_index[:, :, None] * page_rows + jnp.arange(page_rows, dtype=jnp.int32)[None, None, :]
    )
    allowed = owned[:, :, None] & (key_position < cached_lengths[:, None, None])
    allowed = allowed.reshape(page_table.shape[0], slot_count * page_rows)
    scores = (
        jnp.einsum("rhc,kc->rhk", queries, flat_cache, preferred_element_type=jnp.float32)
        * score_scale
    )
    scores = jnp.where(allowed[:, None, :], scores, MASKED)
    peak_score = jnp.max(scores, axis=-1)
    weights = jnp.where(allowed[:, None, :], jnp.exp(scores - peak_score[..., None]), 0.0)
    weight_sum = jnp.sum(weights, axis=-1)
    summed = jnp.einsum(
        "rhk,kl->rhl",
        weights.astype(jnp.bfloat16),
        flat_cache[:, :LAT],
        preferred_element_type=jnp.float32,
    )
    return (peak_score, weight_sum, summed)


def combine_partial(first_state, second_state):
    peak_score = jnp.maximum(first_state[0], second_state[0])
    first_factor = jnp.exp(first_state[0] - peak_score)
    second_factor = jnp.exp(second_state[0] - peak_score)
    weight_sum = first_state[1] * first_factor + second_state[1] * second_factor
    summed = first_state[2] * first_factor[..., None] + second_state[2] * second_factor[..., None]
    return (peak_score, weight_sum, summed)


def on_device(
    prompt_rows,
    step_rows,
    attn_gain,
    latent_gain,
    joined_qkva,
    kv_up,
    out_proj,
    latent_cache,
    page_table,
    cached_lengths,
):
    prompt_count = prompt_rows.shape[0]
    mp_index = lax.axis_index("mp")
    mp_size = lax.axis_size("mp")
    score_scale = (DN + DR) ** (-0.5)
    trainer = (
        joined_qkva.astype(jnp.bfloat16),
        kv_up.astype(jnp.bfloat16),
        out_proj.astype(jnp.bfloat16),
    )
    step_full = lax.all_gather(step_rows, "mp", axis=1, tiled=True)
    stacked = jnp.concatenate([prompt_rows, step_full], axis=0)
    normed = rms_scale(stacked, attn_gain).astype(jnp.bfloat16)
    prompt_ids = jnp.arange(prompt_count, dtype=jnp.int32)
    positions = jnp.concatenate([prompt_ids % LEN, cached_lengths], axis=0)
    served = (
        lax.all_to_all(trainer[0], "mp", split_axis=0, concat_axis=1, tiled=True),
        lax.all_to_all(trainer[1], "mp", split_axis=0, concat_axis=1, tiled=True),
        lax.all_to_all(trainer[2], "mp", split_axis=0, concat_axis=1, tiled=True),
    )
    inputs = normed
    projected = jnp.dot(
        inputs,
        lax.all_gather(served[0], ("dp", "mp"), axis=0, tiled=True),
        preferred_element_type=jnp.float32,
    )
    up_full = lax.all_gather(served[1], ("dp", "mp"), axis=0, tiled=True)
    up_heads = up_full.reshape(LAT, H, DN + DV)
    queries, key_rows = queries_keys(
        projected.astype(jnp.bfloat16), positions, latent_gain, up_heads
    )
    prompt_queries = queries[:prompt_count]
    prompt_key_rows = key_rows[:prompt_count]
    step_queries = queries[prompt_count:]
    step_keys = key_rows[prompt_count:]
    prompt_latent = prompt_attention(
        prompt_queries, prompt_ids, prompt_key_rows, prompt_ids, score_scale
    )
    partial_state = page_attention(
        step_queries, latent_cache, page_table, cached_lengths, mp_index, score_scale
    )
    peak_score, weight_sum, summed = merged(partial_state, "mp", combine_partial)
    own_score = (
        jnp.einsum("rhc,rc->rh", step_queries, step_keys, preferred_element_type=jnp.float32)
        * score_scale
    )
    new_peak = jnp.maximum(peak_score, own_score)
    old_factor = jnp.exp(peak_score - new_peak)
    own_weight = jnp.exp(own_score - new_peak)
    weight_sum = weight_sum * old_factor + own_weight
    own_latent = step_keys[:, :LAT].astype(jnp.float32)
    own_half = own_weight.astype(jnp.bfloat16).astype(jnp.float32)
    summed = summed * old_factor[..., None] + own_half[..., None] * own_latent[:, None, :]
    step_latent = (summed / weight_sum[..., None]).astype(jnp.bfloat16)
    latent_out = jnp.concatenate([prompt_latent, step_latent], axis=0)
    heads_out = jnp.einsum(
        "rhl,lhv->rhv", latent_out, up_heads[..., DN:], preferred_element_type=jnp.float32
    ).astype(jnp.bfloat16)
    heads_out = heads_out.reshape(latent_out.shape[0], H * DV)
    inputs = heads_out
    attended = jnp.dot(
        inputs,
        lax.all_gather(served[2], ("dp", "mp"), axis=0, tiled=True),
        preferred_element_type=jnp.float32,
    )
    attended = attended.astype(jnp.bfloat16)
    prompt_out = attended[:prompt_count]
    col_width = attended.shape[1] // mp_size
    step_out = lax.dynamic_slice_in_dim(attended[prompt_count:], mp_index * col_width, col_width, 1)
    return (prompt_out, step_out)


def solution(mesh):
    placed = (
        P(("dp", "mp"), None),
        P("dp", "mp"),
        P(),
        P(),
        P("dp", "mp"),
        P("dp", "mp"),
        P("dp", "mp"),
        P(("dp", "mp"), None, None),
        P("dp", None),
        P("dp"),
    )
    return jax.shard_map(
        on_device,
        mesh=mesh,
        in_specs=placed,
        out_specs=(P(("dp", "mp"), None), P("dp", "mp")),
        check_vma=False,
    )
```

profile of v0, /device:TPU:0, one launch (start us, length us, event | category | flops | bytes accessed | tf_op | source)
XLA Modules:
  0.0 377.3 jit_solution(3011314813890151468)
XLA Ops:
  7.3 1.1 convert_element_type.168
  8.4 14.4 %all_to_all.57 = bf16[8,16,512]{2,1,0:T(8,128)(2,1)S(1)} all-to-all(bf16[8,16,512]{2,1,0:T(8,128)(2,1)S(1)} %bitcast.86), channel_id=1, replica_groups=mesh['dp'=4,'mp'=8] {'mp'}, dimensions={0} | all-to-all | bytes 262144 | tf_op jit(solution)/shard_map/all_to_all | solution.py:178
  22.8 0.7 copy.118
  23.5 1.4 copy.78
  24.9 18.5 %all_to_all.58 = bf16[8,64,456]{2,1,0:T(8,128)(2,1)S(1)} all-to-all(bf16[8,64,456]{2,1,0:T(8,128)(2,1)S(1)} %bitcast.80), channel_id=1, replica_groups=mesh['dp'=4,'mp'=8] {'mp'}, dimensions={0} | all-to-all | bytes 933888 | tf_op jit(solution)/shard_map/all_to_all | solution.py:177
  43.5 0.3 copy.79
  43.8 1.5 all_to_all.45
  45.3 0.7 convert_element_type.196
  46.1 3.5 all-to-all-start.2
  49.6 0.1 compare_reduce_fusion
  49.8 0.1 and.70
  49.9 0.1 fusion.44
  50.2 31.7 %all_gather.26 = bf16[4,2048]{1,0:T(4,128)(2,1)S(1)} all-gather(bf16[4,256]{1,0:T(4,128)(2,1)S(1)} %copy-done.11), channel_id=1, replica_groups=mesh['dp'=4,'mp'=8] {'mp'}, dimensions={1}, use_global_device_ids=true | all-gather | bytes 18432 | tf_op jit(solution)/shard_map/all_gather | solution.py:171
  81.9 0.5 fusion.18
  82.5 0.9 fusion.35
  83.4 0.7 copy.119
  84.2 2.5 all-gather.11.cloned.1.call-done
  86.7 6.5 %copy.84 = bf16[512,4096]{0,1:T(8,128)(2,1)} copy(bf16[512,4096]{1,0:T(8,128)(2,1)} %all-gather.11.cloned.1.call-done) | data formatting | bytes 8388608 | tf_op jit(solution)/shard_map/all_gather | solution.py:187
  93.1 103.4 %all-gather.9.cloned.1.call-done = bf16[2048,3648]{1,0:T(8,128)(2,1)} async-done(((bf16[64,3648]{1,0:T(8,128)(2,1)}), bf16[2048,3648]{1,0:T(8,128)(2,1)}) %all-gather.9.cloned.1.call-update) | async-done | bytes 14942224 | tf_op jit(solution)/shard_map/all_gather | solution.py:184
  196.5 15.8 %convolution_convert_fusion = bf16[516,3648]{0,1:T(8,128)(2,1)S(1)} fusion(bf16[2048,3648]{1,0:T(8,128)(2,1)} %all-gather.9.cloned.1.call-done, f32[2048]{0:T(1024)S(1)} %copy-done.13, f32[516]{0:T(1024)S(1)} %add_rsqrt_fusion.1, bf16[4,2048]{1,0:T(4,128)(2,1)S(1)} %all_gather.26, bf16[512,2048]{1,0:T(8,128)(2,1)S(1)} %copy-done.5), kind=kOutput, calls=%fused_computation.27 | convolution fusion | flops 7719458816 | bytes 20830736 | tf_op jit(solution)/shard_map/dot_general | solution.py:182
  212.4 0.3 slice.101
  212.7 1.8 copy-done.4
  214.5 1.2 copy-done.2
  215.7 0.1 slice.104
  215.8 2.0 copy.116
  217.8 2.3 convert_element_type.171
  220.2 0.9 slice_convert_fusion.1
  221.1 0.4 subtract_convert_fusion.1
  221.5 0.1 copy.88
  221.6 0.1 copy.87
  221.7 1.3 fusion.31
  223.0 1.3 fusion.33
  224.4 0.2 copy.107
  224.5 4.9 %subtract_convert_fusion = (bf16[516,16,32]{2,0,1:T(8,128)(2,1)S(1)}, bf16[516,16,32]{2,0,1:T(8,128)(2,1)S(1)}) fusion(f32[516,16,64]{2,0,1:T(8,128)} %convert_element_type.171, f32[516,32]{1,0:T(8,128)S(1)} %copy.88, f32[516,32]{1,0:T(8,128)S(1)} %copy.87), kind=kLoop, calls=%fused_computation.34 | loop fusion | flops 2113536 | bytes 3302400 | tf_op jit(solution)/shard_map/convert.8
  229.4 5.6 %convert_bitcast_fusion = bf16[516,16,512]{2,0,1:T(8,128)(2,1)S(1)} fusion(bf16[516,16,192]{0,2,1:T(8,128)(2,1)} %bitcast.74, bf16[512,16,256]{0,2,1:T(8,128)(2,1)} %bitcast.75), kind=kOutput, calls=%fused_computation.21 | convolution fusion | flops 1086357504 | bytes 13172736 | tf_op jit(solution)/shard_map/rhn,lhn->rhl/dot_general | solution.py:71
  235.1 3.2 copy-done
  238.3 0.3 fusion.67
  238.6 19.2 %all-gather.3 = bf16[8,4,16]{2,1,0:T(4,128)(2,1)S(1)} all-gather(bf16[1,4,16]{2,1,0:T(4,128)(2,1)S(1)} %convert_bitcast_fusion.3), channel_id=2, replica_groups=mesh['dp'=4,'mp'=8] {'mp'}, dimensions={0}, use_global_device_ids=true | all-gather | bytes 1152 | tf_op jit(solution)/shard_map/all_gather | solution.py:23
  257.8 0.2 fusion.43
  257.9 16.5 %all-gather.4 = bf16[8,4,16]{2,1,0:T(4,128)(2,1)S(1)} all-gather(bf16[1,4,16]{2,1,0:T(4,128)(2,1)S(1)} %bitcast.89), channel_id=3, replica_groups=mesh['dp'=4,'mp'=8] {'mp'}, dimensions={0}, use_global_device_ids=true | all-gather | bytes 1152 | tf_op jit(solution)/shard_map/all_gather | solution.py:23
  274.5 0.1 fusion.39
  274.6 0.2 convolution_convert_fusion.2
  274.8 31.3 %all-gather.2 = bf16[32,16,512]{2,1,0:T(8,128)(2,1)S(1)} all-gather(bf16[4,16,512]{2,1,0:T(8,128)(2,1)S(1)} %convolution_convert_fusion.2), channel_id=4, replica_groups=mesh['dp'=4,'mp'=8] {'mp'}, dimensions={0}, use_global_device_ids=true | all-gather | bytes 589824 | tf_op jit(solution)/shard_map/all_gather | solution.py:23
  306.1 1.0 while.23
  306.2 0.1 fusion.78
  306.3 0.1 fusion.78
  306.5 0.1 fusion.78
  306.6 0.1 fusion.78
  306.8 0.1 fusion.78
  306.9 0.1 fusion.78
  307.1 0.1 fusion.78
  307.3 0.1 copy.97
  307.7 0.2 fusion.38
  307.8 7.6 %pad_maximum_fusion = bf16[516,16,576]{2,0,1:T(8,128)(2,1)S(1)} fusion(bf16[516,16,32]{2,0,1:T(8,128)(2,1)} %copy-done.1, bf16[516,16,32]{2,0,1:T(8,128)(2,1)S(1)} %get-tuple-element.222, bf16[516,16,512]{2,0,1:T(8,128)(2,1)} %copy-done), kind=kLoop, calls=%fused_computation.14 | loop fusion | flops 28532736 | bytes 19021824 | tf_op jit(solution)/shard_map/concatenate | solution.py:74
  315.5 10.6 %fusion.5 = f32[512,16,512]{0,2,1:T(8,128)} fusion(bf16[516,16,576]{2,0,1:T(8,128)(2,1)S(1)} %pad_maximum_fusion, bf16[516,576]{0,1:T(8,128)(2,1)S(1)} %pad_maximum_fusion.3), kind=kOutput, calls=%fused_computation.15 | convolution fusion | flops 4831838208 | bytes 27852800 | tf_op jit(solution)/shard_map/while/body/eval_jaxpr/qhc,kc->qhk/dot_general | solution.py:90
  326.1 17.4 %fusion.68 = (f32[512,16]{0,1:T(8,128)S(1)}, bf16[512,16,512]{0,2,1:T(8,128)(2,1)}) fusion(f32[512,16,512]{0,2,1:T(8,128)} %fusion.5, pred[512,512]{0,1:T(8,128)(4,1)S(1)} %copy-done.8), kind=kOutput, calls=%fused_computation.120 | output fusion | flops 33554944 | bytes 25460736 | tf_op jit(solution)/shard_map/while/body/eval_jaxpr/sub | solution.py:97
  343.4 10.2 %divide_convert_fusion = bf16[512,16,512]{2,0,1:T(8,128)(2,1)} fusion(f32[512,16]{0,1:T(8,128)S(1)} %get-tuple-element.233, bf16[512,16,512]{0,2,1:T(8,128)(2,1)} %get-tuple-element.234, bf16[516,512]{0,1:T(8,128)(2,1)S(1)} %fusion.33), kind=kOutput, calls=%fused_computation.10 | convolution fusion | flops 4303355904 | bytes 17334272 | tf_op jit(solution)/shard_map/while/body/eval_jaxpr/qhk,kl->qhl/dot_general | solution.py:99
  353.7 5.8 %convert_bitcast_fusion.1 = bf16[516,16,128]{2,0,1:T(8,128)(2,1)S(1)} fusion(bf16[512,16,256]{0,2,1:T(8,128)(2,1)S(1)} %bitcast.76, bf16[4,16,512]{2,0,1:T(4,128)(2,1)S(1)} %fusion.38, bf16[512,16,512]{2,0,1:T(8,128)(2,1)} %divide_convert_fusion), kind=kOutput, calls=%fused_computation.38 | convolution fusion | flops 1100095488 | bytes 12664832 | tf_op jit(solution)/shard_map/rhl,lhv->rhv/dot_general | solution.py:216
  359.5 0.3 copy.100
  359.8 0.4 pad.18
  360.2 0.6 copy.120
  360.8 7.9 %convolution_convert_fusion.1 = bf16[516,2048]{1,0:T(8,128)(2,1)S(1)} fusion(bf16[516,2048]{1,0:T(8,128)(2,1)S(1)} %bitcast.78, bf16[2048,2048]{1,0:T(8,128)(2,1)} %all-gather.13.cloned.1.call-done), kind=kOutput, calls=%fused_computation.35 | convolution fusion | flops 4329578496 | bytes 12615680 | tf_op jit(solution)/shard_map/dot_general | solution.py:221
  368.7 1.5 slice.120
  370.2 0.6 constant_dynamic-slice_fusion.1
  (67 shorter events, 1.4 us)
Async XLA Ops:
  7.2 38.1 %copy-start.7 = (f32[512,256]{1,0:T(8,128)S(1)}, f32[512,256]{1,0:T(8,128)}, u32[]{:S(2)}) copy-start(f32[512,256]{1,0:T(8,128)} %param.18) | copy-start | bytes 1572868
  7.2 42.5 %copy-start.9 = (s32[4,8]{1,0:T(4,128)S(1)}, s32[4,8]{1,0:T(4,128)}, u32[]{:S(2)}) copy-start(s32[4,8]{1,0:T(4,128)} %param.20) | copy-start | bytes 388
  7.2 43.1 %copy-start.11 = (bf16[4,256]{1,0:T(4,128)(2,1)S(1)}, bf16[4,256]{1,0:T(4,128)(2,1)}, u32[]{:S(2)}) copy-start(bf16[4,256]{1,0:T(4,128)(2,1)} %param.13) | copy-start | bytes 6148
  7.2 74.7 %copy-start.12 = (s32[4]{0:T(128)S(1)}, s32[4]{0:T(128)}, u32[]{:S(2)}) copy-start(s32[4]{0:T(128)} %param.21) | copy-start | bytes 52
  7.2 74.7 %copy-start.5 = (bf16[512,2048]{1,0:T(8,128)(2,1)S(1)}, bf16[512,2048]{1,0:T(8,128)(2,1)}, u32[]{:S(2)}) copy-start(bf16[512,2048]{1,0:T(8,128)(2,1)} %param.12) | copy-start | bytes 6291460
  7.2 79.5 %all-gather.11.cloned.1.call-start = ((), (), s32[]{:S(2)}) async-start(), calls=%async_computation.4 | async-start | bytes 4325376 | tf_op jit(solution)/shard_map/all_gather | solution.py:187
  23.5 173.0 %all-gather.9.cloned.1.call-start = ((), (), s32[]{:S(2)}) async-start(), calls=%async_computation.3 | async-start | bytes 15679488 | tf_op jit(solution)/shard_map/all_gather | solution.py:184
  46.1 37.4 %all-to-all-start.2 = ((bf16[8,64,256]{2,1,0:T(8,128)(2,1)}), bf16[8,64,256]{2,1,0:T(8,128)(2,1)S(1)}, u32[]{:S(2)}, u32[]{:S(2)}) async-start(bf16[8,64,256]{2,1,0:T(8,128)(2,1)} %bitcast.25), calls=%async_computation.2 | async-start | bytes 524288 | tf_op jit(solution)/shard_map/all_to_all | solution.py:179
  49.6 311.2 %all-gather.13.cloned.1.call-start = ((), (), s32[]{:S(2)}) async-start(), calls=%async_computation.5 | async-start | bytes 8650752 | tf_op jit(solution)/shard_map/all_gather | solution.py:223
  84.2 112.3 %copy-start.13 = (f32[2048]{0:T(1024)S(1)}, f32[2048]{0:T(1024)}, u32[]{:S(2)}) copy-start(f32[2048]{0:T(1024)} %param.14) | copy-start | bytes 24580
  212.3 2.1 copy-start.4
  212.7 3.0 copy-start.2
  217.8 5.2 %copy-start.10 = (f32[512]{0:T(512)S(1)}, f32[512]{0:T(512)}, u32[]{:S(2)}) copy-start(f32[512]{0:T(512)} %param.15) | copy-start | bytes 6148
  229.4 5.6 %copy-start.1 = (bf16[516,16,32]{2,0,1:T(8,128)(2,1)}, bf16[516,16,32]{2,0,1:T(8,128)(2,1)S(1)}, u32[]{:S(2)}) copy-start(bf16[516,16,32]{2,0,1:T(8,128)(2,1)S(1)} %get-tuple-element.223) | copy-start | bytes 1585156
  235.0 3.3 copy-start
  235.0 3.3 copy-start.6
  315.4 10.6 %copy-start.8 = (pred[512,512]{0,1:T(8,128)(4,1)S(1)}, pred[512,512]{0,1:T(8,128)(4,1)}, u32[]{:S(2)}) copy-start(pred[512,512]{0,1:T(8,128)(4,1)} %fusion.35) | copy-start | bytes 786436
  343.4 10.2 %copy-start.3 = (bf16[512,4096]{0,1:T(8,128)(2,1)S(1)}, bf16[512,4096]{0,1:T(8,128)(2,1)}, u32[]{:S(2)}) copy-start(bf16[512,4096]{0,1:T(8,128)(2,1)} %copy.84) | copy-start | bytes 12582916
Sparse Core Ops, SparseCore 0:
  23.6 63.0 all-gather.10
  90.2 106.2 all-gather.8
  199.5 76.3 all-gather.12
where the time goes:
time: 378 us; the launch traced here: 377 us
  blocking collectives  132 us (35%)
  waiting for transfers between devices  106 us (28%)
  matrix products  56.7 us (15%)
  other arithmetic  41 us (11%)
  local copies, waits for them, and re-layouts  24.1 us (6%)
  between operations  14.1 us (4%)
    all_gather x1, waiting for transfers between devices, on_device(): lax.all_gather(served[0], ('dp', 'mp'), axis=0, tiled=True)  103 us
    all_gather x3, blocking collectives, merged(): lax.all_gather(part.astype(kind), axis)  67 us
    all_gather x1, blocking collectives, on_device(): step_full = lax.all_gather(step_rows, 'mp', axis=1, tiled=True)  31.7 us
    all_to_all x1, blocking collectives, on_device(): lax.all_to_all(trainer[0], 'mp', split_axis=0, concat_axis=1, tiled=True)  18.5 us
    sub x1, other arithmetic, one_block(): weights = jnp.where(allowed[:, None, :], jnp.exp(scores - peak_score), 0.0)  17.4 us
    dot_general x1, matrix products, on_device(): jnp.dot(inputs, lax.all_gather(served[0], ('dp', 'mp'), axis=0, tiled=Tru...  15.8 us
    all_to_all x1, blocking collectives, on_device(): lax.all_to_all(trainer[1], 'mp', split_axis=0, concat_axis=1, tiled=True)  14.4 us
    dot_general x1, matrix products, one_block(): jnp.einsum('qhc,kc->qhk', query_part, all_keys, preferred_element_type=jn...  10.6 us
  transfers between devices with their start and end apart: 4, of which 2 were waited for; matrix products, arithmetic and copies ran while one was open for 27% of the time, Pallas kernels for 0%

commit v1 on v0

--- a/solution.py
+++ b/solution.py
@@ -1,8 +1,11 @@
+import functools
 import math
 
 import jax
 import jax.numpy as jnp
 from jax import lax
+from jax.experimental import pallas as pl
+from jax.experimental.pallas import tpu as pltpu
 from jax.sharding import PartitionSpec as P
 
 H = 16
@@ -230,6 +233,431 @@
     return (prompt_out, step_out)
 
 
+MESH = pl.DeviceIdType.MESH
+STEP_LANES = 128
+STEP_ROWS = 16
+NN = (((1,), (0,)), ((), ()))
+NT = (((1,), (1,)), ((), ()))
+
+
+def mxu(a, b, dims=NN):
+    return lax.dot_general(a, b, dims, preferred_element_type=jnp.float32)
+
+
+def fused_kernel(
+    sizes,
+    x_ref,
+    step_ref,
+    gain_ref,
+    lat_gain_ref,
+    joined_ref,
+    up_ref,
+    out_w_ref,
+    cache_ref,
+    cos_ref,
+    sin_ref,
+    bias_ref,
+    out_ref,
+    step_out_ref,
+    jbuf,
+    ubuf,
+    obuf,
+    sbuf,
+    cbuf,
+    normed,
+    proj,
+    lat_t,
+    keys,
+    q_steps,
+    heads,
+    send_sem,
+    recv_sem,
+    small_send,
+    small_recv,
+):
+    rows, dp_size, mp_size, block_cols, z_size = sizes
+    dp = lax.axis_index("dp")
+    mp = lax.axis_index("mp")
+    x, core = dp // 2, dp % 2
+    z, y = mp // 2, mp % 2
+    bufs = (jbuf, ubuf, obuf)
+    pad_cols = jbuf.shape[1]
+    j_cut = (pad_cols // 32) * 16 + (16 if (pad_cols // 16) % 2 else 0)
+    cuts = ((0, j_cut, pad_cols), (0, 64, 128), (0, 256, 512))
+    d_model = normed.shape[1]
+    depth = d_model // dp_size
+
+    def dev(xx, cc, yy, zz):
+        return (xx * 2 + cc, zz * 2 + yy)
+
+    def slot_of(xx, cc, yy, zz):
+        return (xx * 2 + cc) * mp_size + zz * 2 + yy
+
+    me = slot_of(x, core, y, z)
+    y_dev = dev(x, core, 1 - y, z)
+    x_dev = dev(1 - x, core, y, z)
+    core_dev = dev(x, 1 - core, y, z)
+
+    def z_of(j):
+        return lax.rem(z + 1 + j, z_size)
+
+    barrier = pltpu.get_barrier_semaphore()
+    friends = [dev(x, core, y, z_of(j)) for j in range(z_size - 1)] + [y_dev, x_dev, core_dev]
+    for friend in friends:
+        pl.semaphore_signal(barrier, inc=1, device_id=friend, device_id_type=MESH)
+
+    def copy(t, hf, slot, index, target):
+        lo, hi = cuts[t][hf], cuts[t][hf + 1]
+        ref = bufs[t].at[slot, pl.ds(lo, hi - lo)]
+        return pltpu.make_async_remote_copy(
+            src_ref=ref,
+            dst_ref=ref,
+            send_sem=send_sem.at[t, hf, index],
+            recv_sem=recv_sem.at[t, hf, slot],
+            device_id=target,
+            device_id_type=MESH,
+        )
+
+    def arrived(t, hf, slot):
+        copy(t, hf, slot, 0, core_dev).wait_recv()
+
+    axis_devs = ((y_dev, x_dev), (x_dev, y_dev))
+
+    def begin(t):
+        for hf in range(2):
+            for j in range(z_size - 1):
+                copy(t, hf, me, j, dev(x, core, y, z_of(j))).start()
+            copy(t, hf, me, 3, axis_devs[hf][0]).start()
+            copy(t, hf, me, 7, axis_devs[hf][1]).start()
+            copy(t, hf, me, 15, core_dev).start()
+
+    def near(hf, zz, first, second):
+        if hf == 0:
+            return slot_of(second, core, first, zz)
+        return slot_of(first, core, second, zz)
+
+    def event(t, e):
+        @pl.when(e < 3)
+        def _():
+            for hf in range(2):
+                slot = slot_of(x, core, y, z_of(e))
+                arrived(t, hf, slot)
+                copy(t, hf, slot, 4 + e, axis_devs[hf][0]).start()
+                copy(t, hf, slot, 8 + e, axis_devs[hf][1]).start()
+                copy(t, hf, slot, 16 + e, core_dev).start()
+
+        @pl.when((e >= 3) & (e < 7))
+        def _():
+            j = e - 3
+            zz = lax.rem(z + j, z_size)
+            for hf in range(2):
+                slot = near(hf, zz, 1 - (y, x)[hf], (x, y)[hf])
+                arrived(t, hf, slot)
+                copy(t, hf, slot, 11 + j, axis_devs[hf][1]).start()
+                copy(t, hf, slot, 19 + j, core_dev).start()
+
+        @pl.when((e >= 7) & (e < 15))
+        def _():
+            j = e - 7
+            zz = lax.rem(z + j, z_size)
+            for hf in range(2):
+                first = lax.rem((y, x)[hf] + j // z_size, 2)
+                slot = near(hf, zz, first, 1 - (x, y)[hf])
+                arrived(t, hf, slot)
+                copy(t, hf, slot, 23 + j, core_dev).start()
+
+    def small(k, slot, index, target):
+        ref = (sbuf, cbuf)[k].at[slot]
+        return pltpu.make_async_remote_copy(
+            src_ref=ref,
+            dst_ref=ref,
+            send_sem=small_send.at[k, index],
+            recv_sem=small_recv.at[k, slot],
+            device_id=target,
+            device_id_type=MESH,
+        )
+
+    def small_begin(k):
+        for j in range(z_size - 1):
+            small(k, mp, j, dev(x, core, y, z_of(j))).start()
+        small(k, mp, 3, y_dev).start()
+
+    def small_forward(k):
+        for j in range(z_size - 1):
+            slot = z_of(j) * 2 + y
+            small(k, slot, 0, y_dev).wait_recv()
+            small(k, slot, 4 + j, y_dev).start()
+
+    def small_finish(k):
+        for j in range(z_size):
+            slot = lax.rem(z + j, z_size) * 2 + 1 - y
+            small(k, slot, 0, y_dev).wait_recv()
+
+    jbuf[me] = joined_ref[...]
+    sbuf[mp] = step_ref[...]
+    pl.semaphore_wait(barrier, len(friends))
+    small_begin(0)
+    begin(0)
+
+    for hh in range(2):
+        base = hh * (DN + DV)
+        ubuf[me, :, base : base + DN] = up_ref[:, base : base + DN].astype(jnp.bfloat16)
+        ubuf[me, :, base + DN : base + DN + DV] = (
+            up_ref[:, base + DN : base + DN + DV].T.astype(jnp.bfloat16)
+        )
+    obuf[me] = out_w_ref[...].astype(jnp.bfloat16)
+    cbuf[mp] = cache_ref[...]
+    small_forward(0)
+
+    @pl.loop(0, rows // 64)
+    def _(i):
+        at = pl.ds(pl.multiple_of(i * 64, 64), 64)
+        normed[at, :] = rms_scale(x_ref[at, :], gain_ref[...]).astype(jnp.bfloat16)
+
+    small_finish(0)
+    step_full = jnp.concatenate([sbuf[m] for m in range(mp_size)], axis=1)
+    normed[rows : rows + STEP_ROWS, :] = rms_scale(step_full, gain_ref[...]).astype(jnp.bfloat16)
+    normed[rows + STEP_ROWS :, :] = jnp.zeros(
+        (STEP_LANES - STEP_ROWS, d_model), jnp.bfloat16
+    )
+
+    @pl.loop(0, 7)
+    def _(e):
+        event(0, e)
+
+    begin(1)
+    small_begin(1)
+
+    @pl.loop(7, 15)
+    def _(e):
+        event(0, e)
+
+    small_forward(1)
+
+    def sibling_arrived(t, m):
+        for xx in range(2):
+            for hf in range(2):
+                arrived(t, hf, (xx * 2 + 1 - core) * mp_size + m)
+
+    @pl.loop(0, mp_size)
+    def _(m):
+        sibling_arrived(0, m)
+        event(1, 2 * m)
+
+        @pl.when(m == 2)
+        def _():
+            begin(2)
+
+        total = mxu(jbuf[m], normed[:, :depth], NT)
+        for d in range(1, dp_size):
+            total += mxu(jbuf[d * mp_size + m], normed[:, d * depth : (d + 1) * depth], NT)
+        proj[pl.ds(pl.multiple_of(m * block_cols, 8), block_cols), :] = total[:block_cols]
+        event(1, 2 * m + 1)
+
+    head_cols = H * (DN + DR)
+    latent = proj[head_cols : head_cols + LAT, :].astype(jnp.bfloat16).astype(jnp.float32)
+    mean_square = jnp.mean(latent * latent, axis=0, keepdims=True)
+    latent = latent * lax.rsqrt(mean_square + NORM_EPS) * lat_gain_ref[...]
+    lat_t[...] = latent.astype(jnp.bfloat16)
+
+    def turned(part):
+        part = part.astype(jnp.bfloat16).astype(jnp.float32)
+        low, high = part[: DR // 2], part[DR // 2 :]
+        cosine, sine = cos_ref[...], sin_ref[...]
+        return jnp.concatenate(
+            [low * cosine - high * sine, high * cosine + low * sine], axis=0
+        )
+
+    keys[:, :LAT] = latent.T.astype(jnp.bfloat16)
+    keys[:, LAT:] = turned(proj[head_cols + LAT : head_cols + LAT + DR, :]).T.astype(jnp.bfloat16)
+    q_steps[...] = jnp.zeros_like(q_steps)
+    scale2 = (DN + DR) ** (-0.5) * math.log2(math.e)
+    half = rows // 2
+    causal = lax.broadcasted_iota(jnp.int32, (half, half), 0) <= lax.broadcasted_iota(
+        jnp.int32, (half, half), 1
+    )
+
+    def attend(scores, values):
+        peak = jnp.max(scores, axis=0, keepdims=True)
+        weights = jnp.exp2((scores - peak) * scale2)
+        weight_sum = jnp.sum(weights, axis=0, keepdims=True)
+        summed = mxu(values, weights.astype(jnp.bfloat16))
+        return (summed / weight_sum).astype(jnp.bfloat16)
+
+    def uk_uv(m, hh):
+        base = hh * (DN + DV)
+        w_uk = jnp.concatenate(
+            [ubuf[d * mp_size + m, :, base : base + DN] for d in range(dp_size)], axis=0
+        )
+        w_uv_t = jnp.concatenate(
+            [ubuf[d * mp_size + m, :, base + DN : base + DN + DV] for d in range(dp_size)], axis=1
+        )
+        return w_uk, w_uv_t
+
+    @pl.loop(0, mp_size)
+    def _(m):
+        sibling_arrived(1, m)
+        for hh in range(2):
+            event(2, 2 * m + hh)
+            first = pl.multiple_of(m * 2 * (DN + DR), 2 * (DN + DR)) + hh * (DN + DR)
+            first = pl.multiple_of(first, 64)
+            w_uk, w_uv_t = uk_uv(m, hh)
+            nope = proj[pl.ds(first, DN), :].astype(jnp.bfloat16)
+            q_rot = turned(proj[pl.ds(first + DN, DR), :]).astype(jnp.bfloat16)
+            q_lat = mxu(w_uk, nope).astype(jnp.bfloat16)
+            query = jnp.concatenate([q_lat, q_rot], axis=0)
+            q_steps[...] += pltpu.roll(
+                query[:, rows:].astype(jnp.float32), m * 8 + hh * 4, axis=1
+            )
+            scores = mxu(keys[:half, :], query[:, :half])
+            low = attend(jnp.where(causal, scores, MASKED), lat_t[:, :half])
+            top = mxu(keys[:half, :], query[:, half:rows])
+            end = mxu(keys[half:rows, :], query[:, half:rows])
+            scores = jnp.concatenate([top, jnp.where(causal, end, MASKED)], axis=0)
+            high = attend(scores, lat_t[:, :rows])
+            column = pl.ds(pl.multiple_of(m * 2 * DV + hh * DV, DV), DV)
+            heads[:half, column] = mxu(w_uv_t, low).T.astype(jnp.bfloat16)
+            heads[half:rows, column] = mxu(w_uv_t, high).T.astype(jnp.bfloat16)
+
+    small_finish(1)
+    own_keys = keys[rows : rows + STEP_ROWS, :]
+    all_keys = jnp.concatenate([cbuf[m] for m in range(mp_size)] + [own_keys], axis=0)
+    scores = mxu(q_steps[...].T.astype(jnp.bfloat16), all_keys, NT) + bias_ref[...]
+    peak = jnp.max(scores, axis=1, keepdims=True)
+    weights = jnp.exp2((scores - peak) * scale2)
+    weight_sum = jnp.sum(weights, axis=1, keepdims=True)
+    summed = mxu(weights.astype(jnp.bfloat16), all_keys[:, :LAT])
+    step_latent = (summed / weight_sum).astype(jnp.bfloat16)
+    heads[rows:, :] = jnp.zeros((STEP_ROWS, H * DV), jnp.bfloat16)
+    for h in range(H):
+        _, w_uv_t = uk_uv(h // 2, h % 2)
+        part = mxu(step_latent, w_uv_t, NT)
+        padded = jnp.concatenate(
+            [part[4 * h : 4 * h + 4], jnp.zeros((STEP_ROWS - 4, DV), jnp.float32)], axis=0
+        )
+        heads[rows:, h * DV : (h + 1) * DV] = padded.astype(jnp.bfloat16)
+
+    @pl.loop(0, mp_size)
+    def _(m):
+        sibling_arrived(2, m)
+        total = mxu(heads[:, :depth], obuf[m])
+        for d in range(1, dp_size):
+            total += mxu(heads[:, d * depth : (d + 1) * depth], obuf[d * mp_size + m])
+        width = total.shape[1]
+        done = total.astype(jnp.bfloat16)
+        out_ref[:, pl.ds(pl.multiple_of(m * width, width), width)] = done[:rows]
+
+        @pl.when(m == mp)
+        def _():
+            step_out_ref[...] = done[rows:]
+
+    for t in range(3):
+        for hf in range(2):
+
+            @pl.loop(0, 31)
+            def _(i):
+                copy(t, hf, me, i, core_dev).wait_send()
+
+    for k in range(2):
+
+        @pl.loop(0, 7)
+        def _(i):
+            small(k, mp, i, y_dev).wait_send()
+
+
+def fused_device(
+    prompt_rows,
+    step_rows,
+    attn_gain,
+    latent_gain,
+    joined_qkva,
+    kv_up,
+    out_proj,
+    latent_cache,
+    page_table,
+    cached_lengths,
+):
+    rows, d_model = prompt_rows.shape
+    dp_size, mp_size = lax.axis_size("dp"), lax.axis_size("mp")
+    block_cols = joined_qkva.shape[1]
+    pad_cols = -(-block_cols // 16) * 16
+    joined_t = jnp.pad(joined_qkva.T.astype(jnp.bfloat16), ((0, pad_cols - block_cols), (0, 0)))
+    requests = step_rows.shape[0]
+    steps = jnp.pad(step_rows, ((0, STEP_ROWS - requests), (0, 0)))
+    slot_count, page_rows, key_width = latent_cache.shape
+    lanes = rows + STEP_LANES
+
+    positions = jnp.concatenate(
+        [
+            jnp.arange(rows, dtype=jnp.int32),
+            cached_lengths,
+            jnp.zeros((STEP_LANES - requests,), jnp.int32),
+        ]
+    )
+    freq_steps = jnp.arange(DR // 2, dtype=jnp.float32)
+    inv_freqs = jnp.exp(freq_steps * (-2.0 * math.log(ROPE_BASE) / DR))
+    angles = inv_freqs[:, None] * positions.astype(jnp.float32)[None, :]
+
+    matches = page_table[:, :, None] == jnp.arange(slot_count * mp_size, dtype=jnp.int32)
+    owned = jnp.any(matches, axis=1)
+    page_numbers = jnp.arange(page_table.shape[1], dtype=jnp.int32)[None, :, None]
+    page_index = jnp.sum(jnp.where(matches, page_numbers, 0), axis=1)
+    key_position = page_index[:, :, None] * page_rows + jnp.arange(page_rows, dtype=jnp.int32)
+    allowed = owned[:, :, None] & (key_position < cached_lengths[:, None, None])
+    allowed = jnp.concatenate(
+        [allowed.reshape(requests, -1), jnp.eye(requests, STEP_ROWS, dtype=jnp.bool_)], axis=1
+    )
+    bias = jnp.where(allowed, 0.0, MASKED).astype(jnp.float32)
+    bias = jnp.tile(bias, (STEP_LANES // requests, 1))
+
+    sizes = (rows, dp_size, mp_size, block_cols, mp_size // 2)
+    devices = dp_size * mp_size
+    bf16, f32 = jnp.bfloat16, jnp.float32
+    vmem = pl.BlockSpec(memory_space=pltpu.VMEM)
+    prompt_out, step_out = pl.pallas_call(
+        functools.partial(fused_kernel, sizes),
+        out_shape=(
+            jax.ShapeDtypeStruct((rows, d_model), bf16),
+            jax.ShapeDtypeStruct((STEP_ROWS, out_proj.shape[1]), bf16),
+        ),
+        in_specs=[vmem] * 11,
+        out_specs=(vmem, vmem),
+        scratch_shapes=[
+            pltpu.VMEM((devices, pad_cols, joined_qkva.shape[0]), bf16),
+            pltpu.VMEM((devices,) + kv_up.shape, bf16),
+            pltpu.VMEM((devices,) + out_proj.shape, bf16),
+            pltpu.VMEM((mp_size, STEP_ROWS, step_rows.shape[1]), bf16),
+            pltpu.VMEM((mp_size, slot_count * page_rows, key_width), bf16),
+            pltpu.VMEM((lanes, d_model), bf16),
+            pltpu.VMEM((mp_size * block_cols, lanes), f32),
+            pltpu.VMEM((LAT, lanes), bf16),
+            pltpu.VMEM((lanes, LAT + DR), bf16),
+            pltpu.VMEM((LAT + DR, STEP_LANES), f32),
+            pltpu.VMEM((rows + STEP_ROWS, H * DV), bf16),
+            pltpu.SemaphoreType.DMA((3, 2, 31)),
+            pltpu.SemaphoreType.DMA((3, 2, devices)),
+            pltpu.SemaphoreType.DMA((2, 7)),
+            pltpu.SemaphoreType.DMA((2, mp_size)),
+        ],
+        compiler_params=pltpu.CompilerParams(
+            collective_id=0, has_side_effects=True, vmem_limit_bytes=64 * 1024 * 1024
+        ),
+    )(
+        prompt_rows,
+        steps,
+        attn_gain[None, :],
+        latent_gain[:, None],
+        joined_t,
+        kv_up,
+        out_proj,
+        latent_cache.reshape(slot_count * page_rows, key_width),
+        jnp.cos(angles),
+        jnp.sin(angles),
+        bias,
+    )
+    return prompt_out, step_out[:requests]
+
+
 def solution(mesh):
     placed = (
         P(("dp", "mp"), None),
@@ -243,8 +671,9 @@
         P("dp", None),
         P("dp"),
     )
+    fits = mesh.shape["dp"] == 4 and mesh.shape["mp"] == 8
     return jax.shard_map(
-        on_device,
+        fused_device if fits else on_device,
         mesh=mesh,
         in_specs=placed,
         out_specs=(P(("dp", "mp"), None), P("dp", "mp")),

time: 378 us -> 202 us (0.53)
  the two profiles are of different devices: /device:TPU:0 before, /device:TPU:8 now
where the time goes in v1:
time: 202 us; the launch traced here: 201 us
  Pallas kernels  186 us (92%)
  local copies, waits for them, and re-layouts  9.63 us (5%)
  other arithmetic  5.32 us (3%)
    pallas_call x1, Pallas kernels, fused_device(): pl.pallas_call(functools.partial(fused_kernel, sizes), out_shape=(jax.Sha...  186 us

profile of v1, /device:TPU:8, one launch (start us, length us, event | category | flops | bytes accessed | tf_op | source)
XLA Modules:
  0.0 201.5 jit_solution(1861881066438675617)
XLA Ops:
  0.6 0.8 fusion
  1.4 0.8 select_reduce_fusion
  2.2 0.7 add_convert_fusion
  3.0 1.3 pad.8.step_ref
  4.2 0.1 and.13
  4.3 0.1 and.14
  4.5 0.1 add.29
  4.6 0.1 add.26
  4.6 0.1 add.27
  4.8 0.7 fusion.1
  5.5 1.0 multiply_sine_fusion
  6.6 1.5 copy.13.lat_gain_ref
  8.1 1.2 convert_bitcast_fusion
  9.3 0.8 pad.9.joined_ref
  10.1 0.1 tile.4
  10.2 1.0 tile.10.bias_ref
  11.2 185.8 %shard_map.113 = (bf16[512,2048]{1,0:T(8,128)(2,1)}, bf16[16,256]{1,0:T(8,128)(2,1)}) custom-call(bf16[512,2048]{1,0:T(8,128)(2,1)} %x_ref.1, bf16[16,256]{1,0:T(8,128)(2,1)} %pad.8.step_ref, f32[1,2048]{1,0:T(1,128)} %bitcast.6, f32[512,1]{1,0:T(8,128)} %copy.13.lat_gain_ref, bf16[464,512]{1,0:T(8,128)(2,1)} %pad.9.joined_ref, f32[128,512]{1,0:T(8,128)} %up_ref.1, ...), custom_call_target="tpu_custom_call" | custom-call | tf_op jit(solution)/shard_map/pallas_call | solution.py:617
  197.1 1.3 slice.3
  198.3 3.2 %copy.15 = bf16[512,2048]{1,0:T(8,128)(2,1)} copy(bf16[512,2048]{1,0:T(8,128)(2,1)} %get-tuple-element.10) | data formatting | bytes 4194304
  (7 shorter events, 0.0 us)

commit v2 on v1

--- a/solution.py
+++ b/solution.py
@@ -254,9 +254,8 @@
     up_ref,
     out_w_ref,
     cache_ref,
-    cos_ref,
-    sin_ref,
-    bias_ref,
+    table_ref,
+    lengths_ref,
     out_ref,
     step_out_ref,
     jbuf,
@@ -270,22 +269,26 @@
     keys,
     q_steps,
     heads,
+    cosine_s,
+    sine_s,
     send_sem,
     recv_sem,
     small_send,
     small_recv,
 ):
-    rows, dp_size, mp_size, block_cols, z_size = sizes
+    rows, dp_size, mp_size, block_cols, z_size, page_rows = sizes
     dp = lax.axis_index("dp")
     mp = lax.axis_index("mp")
     x, core = dp // 2, dp % 2
     z, y = mp // 2, mp % 2
     bufs = (jbuf, ubuf, obuf)
     pad_cols = jbuf.shape[1]
-    j_cut = (pad_cols // 32) * 16 + (16 if (pad_cols // 16) % 2 else 0)
-    cuts = ((0, j_cut, pad_cols), (0, 64, 128), (0, 256, 512))
-    d_model = normed.shape[1]
-    depth = d_model // dp_size
+    cuts = tuple(
+        (0, (buf.shape[1] * 59 // 1600) * 16, buf.shape[1]) for buf in bufs
+    )
+    depth = normed.shape[2]
+    requests = step_ref.shape[0]
+    lanes = rows + STEP_LANES
 
     def dev(xx, cc, yy, zz):
         return (xx * 2 + cc, zz * 2 + yy)
@@ -393,8 +396,20 @@
             slot = lax.rem(z + j, z_size) * 2 + 1 - y
             small(k, slot, 0, y_dev).wait_recv()
 
-    jbuf[me] = joined_ref[...]
-    sbuf[mp] = step_ref[...]
+    whole_cols = block_cols // 128 * 128
+    rest_cols = block_cols - whole_cols
+    jbuf[me, :whole_cols, :] = joined_ref[:, :whole_cols].T.astype(jnp.bfloat16)
+    rest = jnp.concatenate(
+        [joined_ref[:, whole_cols:], jnp.zeros((depth, 128 - rest_cols), jnp.float32)], axis=1
+    )
+    jbuf[me, whole_cols:, :] = rest.T[: pad_cols - whole_cols].astype(jnp.bfloat16)
+    sbuf[mp] = jnp.concatenate(
+        [
+            step_ref[...].astype(jnp.float32),
+            jnp.zeros((STEP_ROWS - requests, step_ref.shape[1]), jnp.float32),
+        ],
+        axis=0,
+    ).astype(jnp.bfloat16)
     pl.semaphore_wait(barrier, len(friends))
     small_begin(0)
     begin(0)
@@ -412,58 +427,87 @@
     @pl.loop(0, rows // 64)
     def _(i):
         at = pl.ds(pl.multiple_of(i * 64, 64), 64)
-        normed[at, :] = rms_scale(x_ref[at, :], gain_ref[...]).astype(jnp.bfloat16)
+        part = rms_scale(x_ref[at, :], gain_ref[...]).astype(jnp.bfloat16)
+        for d in range(dp_size):
+            normed[d, at, :] = part[:, d * depth : (d + 1) * depth]
+
+    @pl.loop(0, proj.shape[0] // 64)
+    def _(i):
+        proj[pl.ds(pl.multiple_of(i * 64, 64), 64), :] = jnp.zeros((64, lanes), jnp.float32)
 
     small_finish(0)
     step_full = jnp.concatenate([sbuf[m] for m in range(mp_size)], axis=1)
-    normed[rows : rows + STEP_ROWS, :] = rms_scale(step_full, gain_ref[...]).astype(jnp.bfloat16)
-    normed[rows + STEP_ROWS :, :] = jnp.zeros(
-        (STEP_LANES - STEP_ROWS, d_model), jnp.bfloat16
-    )
-
-    @pl.loop(0, 7)
-    def _(e):
-        event(0, e)
-
-    begin(1)
-    small_begin(1)
-
-    @pl.loop(7, 15)
-    def _(e):
-        event(0, e)
-
+    part = rms_scale(step_full, gain_ref[...]).astype(jnp.bfloat16)
+    for d in range(dp_size):
+        normed[d, rows : rows + STEP_ROWS, :] = part[:, d * depth : (d + 1) * depth]
+        normed[d, rows + STEP_ROWS :, :] = jnp.zeros((STEP_LANES - STEP_ROWS, depth), jnp.bfloat16)
+
+    def slot_at(hf, n, cc):
+        zz = lax.rem(z + n, z_size)
+        first = lax.rem((y, x)[hf] + n // 4, 2)
+        second = lax.rem((x, y)[hf] + n // 8, 2)
+        if hf == 0:
+            return slot_of(second, cc, first, zz)
+        return slot_of(first, cc, second, zz)
+
+    def project(n, cc, wait):
+        for hf in range(2):
+            slot = slot_at(hf, n, cc)
+            if wait:
+                arrived(0, hf, slot)
+            lo, hi = cuts[0][hf], cuts[0][hf + 1]
+            valid = min(hi, block_cols) - lo
+            total = mxu(jbuf[slot, lo:hi, :], normed[slot // mp_size], NT)
+            at = pl.ds(pl.multiple_of(lax.rem(slot, mp_size) * block_cols + lo, 8), valid)
+            proj[at, :] += total[:valid]
+
+    project(0, core, False)
+
+    @pl.loop(1, 16)
+    def _(n):
+        event(0, n - 1)
+
+        @pl.when(n == 7)
+        def _():
+            begin(1)
+            small_begin(1)
+
+        @pl.when(n >= 12)
+        def _():
+            event(1, n - 12)
+
+        project(n, core, False)
+        project(n - 1, 1 - core, True)
+
+    begin(2)
     small_forward(1)
+    project(15, 1 - core, True)
 
     def sibling_arrived(t, m):
         for xx in range(2):
             for hf in range(2):
                 arrived(t, hf, (xx * 2 + 1 - core) * mp_size + m)
 
-    @pl.loop(0, mp_size)
-    def _(m):
-        sibling_arrived(0, m)
-        event(1, 2 * m)
-
-        @pl.when(m == 2)
-        def _():
-            begin(2)
-
-        total = mxu(jbuf[m], normed[:, :depth], NT)
-        for d in range(1, dp_size):
-            total += mxu(jbuf[d * mp_size + m], normed[:, d * depth : (d + 1) * depth], NT)
-        proj[pl.ds(pl.multiple_of(m * block_cols, 8), block_cols), :] = total[:block_cols]
-        event(1, 2 * m + 1)
+    lane = lax.broadcasted_iota(jnp.int32, (DR // 2, lanes), 1)
+    positions = jnp.where(lane < rows, lane, 0)
+    for r in range(requests):
+        positions = jnp.where(lane == rows + r, lengths_ref[r], positions)
+    step = lax.broadcasted_iota(jnp.int32, (DR // 2, lanes), 0).astype(jnp.float32)
+    angles = positions.astype(jnp.float32) * jnp.exp(step * (-2.0 * math.log(ROPE_BASE) / DR))
+    cosine_s[...] = jnp.cos(angles)
+    sine_s[...] = jnp.sin(angles)
 
     head_cols = H * (DN + DR)
     latent = proj[head_cols : head_cols + LAT, :].astype(jnp.bfloat16).astype(jnp.float32)
     mean_square = jnp.mean(latent * latent, axis=0, keepdims=True)
-    latent = latent * lax.rsqrt(mean_square + NORM_EPS) * lat_gain_ref[...]
+    lat_gain = jnp.broadcast_to(lat_gain_ref[...], (8, LAT)).T[:, :1]
+    latent = latent * lax.rsqrt(mean_square + NORM_EPS) * lat_gain
     lat_t[...] = latent.astype(jnp.bfloat16)
 
     def turned(part):
         part = part.astype(jnp.bfloat16).astype(jnp.float32)
         low, high = part[: DR // 2], part[DR // 2 :]
-        cosine, sine = cos_ref[...], sin_ref[...]
+        cosine, sine = cosine_s[...], sine_s[...]
         return jnp.concatenate(
             [low * cosine - high * sine, high * cosine + low * sine], axis=0
         )
@@ -494,11 +538,19 @@
         )
         return w_uk, w_uv_t
 
+    @pl.loop(4, 15)
+    def _(e):
+        event(1, e)
+
+        @pl.when(e >= 11)
+        def _():
+            event(2, e - 11)
+
     @pl.loop(0, mp_size)
     def _(m):
         sibling_arrived(1, m)
         for hh in range(2):
-            event(2, 2 * m + hh)
+            event(2, 4 + 2 * m + hh)
             first = pl.multiple_of(m * 2 * (DN + DR), 2 * (DN + DR)) + hh * (DN + DR)
             first = pl.multiple_of(first, 64)
             w_uk, w_uv_t = uk_uv(m, hh)
@@ -522,7 +574,21 @@
     small_finish(1)
     own_keys = keys[rows : rows + STEP_ROWS, :]
     all_keys = jnp.concatenate([cbuf[m] for m in range(mp_size)] + [own_keys], axis=0)
-    scores = mxu(q_steps[...].T.astype(jnp.bfloat16), all_keys, NT) + bias_ref[...]
+    cached = mp_size * cache_ref.shape[0]
+    column = lax.broadcasted_iota(jnp.int32, (8, cached), 1)
+    request = lax.rem(lax.broadcasted_iota(jnp.int32, (8, cached), 0), requests)
+    slot, entry = column // page_rows, lax.rem(column, page_rows)
+    bias = jnp.full((8, cached), MASKED, jnp.float32)
+    for r in range(requests):
+        for page in range(table_ref.shape[1]):
+            counts = (slot == table_ref[r, page]) & (page * page_rows + entry < lengths_ref[r])
+            bias = jnp.where(counts & (request == r), 0.0, bias)
+    own = lax.broadcasted_iota(jnp.int32, (8, STEP_ROWS), 1) == lax.rem(
+        lax.broadcasted_iota(jnp.int32, (8, STEP_ROWS), 0), requests
+    )
+    bias = jnp.concatenate([bias, jnp.where(own, 0.0, MASKED)], axis=1)
+    bias = jnp.concatenate([bias] * (STEP_LANES // 8), axis=0)
+    scores = mxu(q_steps[...].T.astype(jnp.bfloat16), all_keys, NT) + bias
     peak = jnp.max(scores, axis=1, keepdims=True)
     weights = jnp.exp2((scores - peak) * scale2)
     weight_sum = jnp.sum(weights, axis=1, keepdims=True)
@@ -549,7 +615,7 @@
 
         @pl.when(m == mp)
         def _():
-            step_out_ref[...] = done[rows:]
+            step_out_ref[...] = total[rows : rows + requests].astype(jnp.bfloat16)
 
     for t in range(3):
         for hf in range(2):
@@ -581,36 +647,10 @@
     dp_size, mp_size = lax.axis_size("dp"), lax.axis_size("mp")
     block_cols = joined_qkva.shape[1]
     pad_cols = -(-block_cols // 16) * 16
-    joined_t = jnp.pad(joined_qkva.T.astype(jnp.bfloat16), ((0, pad_cols - block_cols), (0, 0)))
     requests = step_rows.shape[0]
-    steps = jnp.pad(step_rows, ((0, STEP_ROWS - requests), (0, 0)))
     slot_count, page_rows, key_width = latent_cache.shape
     lanes = rows + STEP_LANES
-
-    positions = jnp.concatenate(
-        [
-            jnp.arange(rows, dtype=jnp.int32),
-            cached_lengths,
-            jnp.zeros((STEP_LANES - requests,), jnp.int32),
-        ]
-    )
-    freq_steps = jnp.arange(DR // 2, dtype=jnp.float32)
-    inv_freqs = jnp.exp(freq_steps * (-2.0 * math.log(ROPE_BASE) / DR))
-    angles = inv_freqs[:, None] * positions.astype(jnp.float32)[None, :]
-
-    matches = page_table[:, :, None] == jnp.arange(slot_count * mp_size, dtype=jnp.int32)
-    owned = jnp.any(matches, axis=1)
-    page_numbers = jnp.arange(page_table.shape[1], dtype=jnp.int32)[None, :, None]
-    page_index = jnp.sum(jnp.where(matches, page_numbers, 0), axis=1)
-    key_position = page_index[:, :, None] * page_rows + jnp.arange(page_rows, dtype=jnp.int32)
-    allowed = owned[:, :, None] & (key_position < cached_lengths[:, None, None])
-    allowed = jnp.concatenate(
-        [allowed.reshape(requests, -1), jnp.eye(requests, STEP_ROWS, dtype=jnp.bool_)], axis=1
-    )
-    bias = jnp.where(allowed, 0.0, MASKED).astype(jnp.float32)
-    bias = jnp.tile(bias, (STEP_LANES // requests, 1))
-
-    sizes = (rows, dp_size, mp_size, block_cols, mp_size // 2)
+    sizes = (rows, dp_size, mp_size, block_cols, mp_size // 2, page_rows)
     devices = dp_size * mp_size
     bf16, f32 = jnp.bfloat16, jnp.float32
     vmem = pl.BlockSpec(memory_space=pltpu.VMEM)
@@ -618,9 +658,9 @@
         functools.partial(fused_kernel, sizes),
         out_shape=(
             jax.ShapeDtypeStruct((rows, d_model), bf16),
-            jax.ShapeDtypeStruct((STEP_ROWS, out_proj.shape[1]), bf16),
+            jax.ShapeDtypeStruct((requests, out_proj.shape[1]), bf16),
         ),
-        in_specs=[vmem] * 11,
+        in_specs=[vmem] * 8 + [pl.BlockSpec(memory_space=pltpu.SMEM)] * 2,
         out_specs=(vmem, vmem),
         scratch_shapes=[
             pltpu.VMEM((devices, pad_cols, joined_qkva.shape[0]), bf16),
@@ -628,12 +668,14 @@
             pltpu.VMEM((devices,) + out_proj.shape, bf16),
             pltpu.VMEM((mp_size, STEP_ROWS, step_rows.shape[1]), bf16),
             pltpu.VMEM((mp_size, slot_count * page_rows, key_width), bf16),
-            pltpu.VMEM((lanes, d_model), bf16),
+            pltpu.VMEM((dp_size, lanes, joined_qkva.shape[0]), bf16),
             pltpu.VMEM((mp_size * block_cols, lanes), f32),
             pltpu.VMEM((LAT, lanes), bf16),
             pltpu.VMEM((lanes, LAT + DR), bf16),
             pltpu.VMEM((LAT + DR, STEP_LANES), f32),
             pltpu.VMEM((rows + STEP_ROWS, H * DV), bf16),
+            pltpu.VMEM((DR // 2, lanes), f32),
+            pltpu.VMEM((DR // 2, lanes), f32),
             pltpu.SemaphoreType.DMA((3, 2, 31)),
             pltpu.SemaphoreType.DMA((3, 2, devices)),
             pltpu.SemaphoreType.DMA((2, 7)),
@@ -644,18 +686,17 @@
         ),
     )(
         prompt_rows,
-        steps,
+        step_rows,
         attn_gain[None, :],
-        latent_gain[:, None],
-        joined_t,
+        latent_gain[None, :],
+        joined_qkva,
         kv_up,
         out_proj,
         latent_cache.reshape(slot_count * page_rows, key_width),
-        jnp.cos(angles),
-        jnp.sin(angles),
-        bias,
-    )
-    return prompt_out, step_out[:requests]
+        page_table,
+        cached_lengths,
+    )
+    return prompt_out, step_out
 
 
 def solution(mesh):

time: 202 us -> 190 us (0.941)
  other arithmetic: 5.32 us -> 0 us
  local copies, waits for them, and re-layouts: 9.63 us -> 6.23 us
  Pallas kernels: 186 us -> 183 us
    unnamed x1 -> x5, local copies, waits for them, and re-layouts: 3.16 us -> 6.23 us
    pallas_call x1, Pallas kernels: 186 us -> 183 us  [fused_device(): pl.pallas_call(functools.partial(fused_kernel, sizes), out_shape=(jax.Sha...]
    pad x2 -> x0, local copies, waits for them, and re-layouts: 2.08 us -> none  [the longest x1 1.28 us: fused_device(): steps = jnp.pad(step_rows, ((0, STEP_ROWS - requests), (0, 0)))]
where the time goes in v2:
time: 190 us
  Pallas kernels  183 us (96%)
  local copies, waits for them, and re-layouts  6.23 us (3%)
    pallas_call x1, Pallas kernels, fused_device(): pl.pallas_call(functools.partial(fused_kernel, sizes), out_shape=(jax.Sha...  183 us
    unnamed x5, local copies, waits for them, and re-layouts  6.23 us

profile of v2, /device:TPU:8, one launch (start us, length us, event | category | flops | bytes accessed | tf_op | source)
XLA Modules:
  0.0 189.9 jit_solution(16547882050591761174)
XLA Ops:
  0.6 2.5 %copy.12.joined_ref = f32[512,456]{1,0:T(8,128)} copy(f32[512,456]{0,1:T(8,128)} %param.14) | data formatting | bytes 1867776 | tf_op args[4]
  3.1 183.0 %shard_map.113 = (bf16[512,2048]{1,0:T(8,128)(2,1)}, bf16[4,256]{1,0:T(4,128)(2,1)}) custom-call(bf16[512,2048]{1,0:T(8,128)(2,1)} %x_ref.1, bf16[4,256]{1,0:T(4,128)(2,1)} %step_ref.1, f32[1,2048]{1,0:T(1,128)} %bitcast.4, f32[1,512]{1,0:T(1,128)} %bitcast.5, f32[512,456]{1,0:T(8,128)} %copy.12.joined_ref, f32[128,512]{1,0:T(8,128)} %up_ref.1, ...), custom_call_target="tpu_custom_call" | custom-call | tf_op jit(solution)/shard_map/pallas_call | solution.py:657
  186.1 0.0 copy-start
  186.1 3.2 %copy.15 = bf16[512,2048]{1,0:T(8,128)(2,1)} copy(bf16[512,2048]{1,0:T(8,128)(2,1)} %get-tuple-element.4) | data formatting | bytes 4194304
  189.3 0.0 copy-done
  189.3 0.6 copy.16
Async XLA Ops:
  186.1 3.2 %copy-start = (bf16[4,256]{1,0:T(4,128)(2,1)S(1)}, bf16[4,256]{1,0:T(4,128)(2,1)}, u32[]{:S(2)}) copy-start(bf16[4,256]{1,0:T(4,128)(2,1)} %get-tuple-element.5) | copy-start | bytes 6148

commit v3 on v2

--- a/solution.py
+++ b/solution.py
@@ -301,13 +301,35 @@
     x_dev = dev(1 - x, core, y, z)
     core_dev = dev(x, 1 - core, y, z)
 
-    def z_of(j):
-        return lax.rem(z + 1 + j, z_size)
+    middle = (z == 1) | (z == 2)
+
+    def z_at(n):
+        far = z // 2
+        inner = lax.rem(lax.rem(z + 1, z_size) // 2, 2)
+        place = (1 - inner) * n + inner * (lax.rem(n + 1, 3) + n // 3 * 2)
+        return (1 - far) * place + far * (z_size - 1 - place)
+
+    def z_next(e):
+        odd = lax.rem(e, 2)
+        return dev(x, core, y, (1 - odd) * 3 * (z - 1) + odd * (3 - z))
+
+    def z_neighbours(act):
+        @pl.when(z > 0)
+        def _():
+            act(0, dev(x, core, y, z - 1))
+
+        @pl.when(z < z_size - 1)
+        def _():
+            act(1, dev(x, core, y, z + 1))
 
     barrier = pltpu.get_barrier_semaphore()
-    friends = [dev(x, core, y, z_of(j)) for j in range(z_size - 1)] + [y_dev, x_dev, core_dev]
-    for friend in friends:
+
+    def greet(_, friend):
         pl.semaphore_signal(barrier, inc=1, device_id=friend, device_id_type=MESH)
+
+    z_neighbours(greet)
+    for friend in (y_dev, x_dev, core_dev):
+        greet(None, friend)
 
     def copy(t, hf, slot, index, target):
         lo, hi = cuts[t][hf], cuts[t][hf + 1]
@@ -328,8 +350,7 @@
 
     def begin(t):
         for hf in range(2):
-            for j in range(z_size - 1):
-                copy(t, hf, me, j, dev(x, core, y, z_of(j))).start()
+            z_neighbours(lambda i, target: copy(t, hf, me, i, target).start())
             copy(t, hf, me, 3, axis_devs[hf][0]).start()
             copy(t, hf, me, 7, axis_devs[hf][1]).start()
             copy(t, hf, me, 15, core_dev).start()
@@ -343,8 +364,13 @@
         @pl.when(e < 3)
         def _():
             for hf in range(2):
-                slot = slot_of(x, core, y, z_of(e))
+                slot = slot_of(x, core, y, z_at(e + 1))
                 arrived(t, hf, slot)
+
+                @pl.when(middle)
+                def _():
+                    copy(t, hf, slot, 31 + e, z_next(e)).start()
+
                 copy(t, hf, slot, 4 + e, axis_devs[hf][0]).start()
                 copy(t, hf, slot, 8 + e, axis_devs[hf][1]).start()
                 copy(t, hf, slot, 16 + e, core_dev).start()
@@ -352,7 +378,7 @@
         @pl.when((e >= 3) & (e < 7))
         def _():
             j = e - 3
-            zz = lax.rem(z + j, z_size)
+            zz = z_at(j)
             for hf in range(2):
                 slot = near(hf, zz, 1 - (y, x)[hf], (x, y)[hf])
                 arrived(t, hf, slot)
@@ -362,7 +388,7 @@
         @pl.when((e >= 7) & (e < 15))
         def _():
             j = e - 7
-            zz = lax.rem(z + j, z_size)
+            zz = z_at(lax.rem(j, z_size))
             for hf in range(2):
                 first = lax.rem((y, x)[hf] + j // z_size, 2)
                 slot = near(hf, zz, first, 1 - (x, y)[hf])
@@ -381,28 +407,28 @@
         )
 
     def small_begin(k):
-        for j in range(z_size - 1):
-            small(k, mp, j, dev(x, core, y, z_of(j))).start()
-        small(k, mp, 3, y_dev).start()
+        z_neighbours(lambda i, target: small(k, mp, i, target).start())
+        small(k, mp, 2, y_dev).start()
 
     def small_forward(k):
-        for j in range(z_size - 1):
-            slot = z_of(j) * 2 + y
+        for e in range(z_size - 1):
+            slot = z_at(e + 1) * 2 + y
             small(k, slot, 0, y_dev).wait_recv()
-            small(k, slot, 4 + j, y_dev).start()
+
+            @pl.when(middle)
+            def _():
+                small(k, slot, 6 + e, z_next(e)).start()
+
+            small(k, slot, 3 + e, y_dev).start()
 
     def small_finish(k):
         for j in range(z_size):
-            slot = lax.rem(z + j, z_size) * 2 + 1 - y
+            slot = z_at(j) * 2 + 1 - y
             small(k, slot, 0, y_dev).wait_recv()
 
-    whole_cols = block_cols // 128 * 128
-    rest_cols = block_cols - whole_cols
-    jbuf[me, :whole_cols, :] = joined_ref[:, :whole_cols].T.astype(jnp.bfloat16)
-    rest = jnp.concatenate(
-        [joined_ref[:, whole_cols:], jnp.zeros((depth, 128 - rest_cols), jnp.float32)], axis=1
-    )
-    jbuf[me, whole_cols:, :] = rest.T[: pad_cols - whole_cols].astype(jnp.bfloat16)
+    jbuf[me] = jnp.concatenate(
+        [joined_ref[...], jnp.zeros((pad_cols - block_cols, depth), jnp.float32)], axis=0
+    ).astype(jnp.bfloat16)
     sbuf[mp] = jnp.concatenate(
         [
             step_ref[...].astype(jnp.float32),
@@ -410,7 +436,7 @@
         ],
         axis=0,
     ).astype(jnp.bfloat16)
-    pl.semaphore_wait(barrier, len(friends))
+    pl.semaphore_wait(barrier, 4 + lax.rem((z + 1) // 2, 2))
     small_begin(0)
     begin(0)
 
@@ -443,7 +469,7 @@
         normed[d, rows + STEP_ROWS :, :] = jnp.zeros((STEP_LANES - STEP_ROWS, depth), jnp.bfloat16)
 
     def slot_at(hf, n, cc):
-        zz = lax.rem(z + n, z_size)
+        zz = z_at(n % 4)
         first = lax.rem((y, x)[hf] + n // 4, 2)
         second = lax.rem((x, y)[hf] + n // 8, 2)
         if hf == 0:
@@ -617,18 +643,28 @@
         def _():
             step_out_ref[...] = total[rows : rows + requests].astype(jnp.bfloat16)
 
+    def z_sent(wait, count):
+        z_neighbours(lambda i, target: wait(i))
+
+        @pl.when(middle)
+        def _():
+            for e in range(z_size - 1):
+                wait(count + e)
+
     for t in range(3):
         for hf in range(2):
-
-            @pl.loop(0, 31)
+            sent = lambda i: copy(t, hf, me, i, core_dev).wait_send()
+            z_sent(sent, 31)
+
+            @pl.loop(3, 31)
             def _(i):
-                copy(t, hf, me, i, core_dev).wait_send()
+                sent(i)
 
     for k in range(2):
-
-        @pl.loop(0, 7)
-        def _(i):
-            small(k, mp, i, y_dev).wait_send()
+        sent = lambda i: small(k, mp, i, y_dev).wait_send()
+        z_sent(sent, 6)
+        for i in range(2, 6):
+            sent(i)
 
 
 def fused_device(
@@ -676,9 +712,9 @@
             pltpu.VMEM((rows + STEP_ROWS, H * DV), bf16),
             pltpu.VMEM((DR // 2, lanes), f32),
             pltpu.VMEM((DR // 2, lanes), f32),
-            pltpu.SemaphoreType.DMA((3, 2, 31)),
+            pltpu.SemaphoreType.DMA((3, 2, 34)),
             pltpu.SemaphoreType.DMA((3, 2, devices)),
-            pltpu.SemaphoreType.DMA((2, 7)),
+            pltpu.SemaphoreType.DMA((2, 9)),
             pltpu.SemaphoreType.DMA((2, mp_size)),
         ],
         compiler_params=pltpu.CompilerParams(
@@ -689,7 +725,7 @@
         step_rows,
         attn_gain[None, :],
         latent_gain[None, :],
-        joined_qkva,
+        joined_qkva.T,
         kv_up,
         out_proj,
         latent_cache.reshape(slot_count * page_rows, key_width),

time: 190 us -> 170 us (0.89)
  the two profiles are of different devices: /device:TPU:8 before, /device:TPU:0 now
where the time goes in v3:
time: 170 us
  Pallas kernels  165 us (97%)
  local copies, waits for them, and re-layouts  3.74 us (2%)
    pallas_call x1, Pallas kernels, fused_device(): pl.pallas_call(functools.partial(fused_kernel, sizes), out_shape=(jax.Sha...  165 us
    unnamed x4, local copies, waits for them, and re-layouts  3.74 us

profile of v3, /device:TPU:0, one launch (start us, length us, event | category | flops | bytes accessed | tf_op | source)
XLA Modules:
  0.0 169.7 jit_solution(4558929743223369992)
XLA Ops:
  0.6 165.3 %shard_map.113 = (bf16[512,2048]{1,0:T(8,128)(2,1)}, bf16[4,256]{1,0:T(4,128)(2,1)}) custom-call(bf16[512,2048]{1,0:T(8,128)(2,1)} %x_ref.1, bf16[4,256]{1,0:T(4,128)(2,1)} %step_ref.1, f32[1,2048]{1,0:T(1,128)} %bitcast.6, f32[1,512]{1,0:T(1,128)} %bitcast.7, f32[456,512]{1,0:T(8,128)} %bitcast.4, f32[128,512]{1,0:T(8,128)} %up_ref.1, ...), custom_call_target="tpu_custom_call" | custom-call | tf_op jit(solution)/shard_map/pallas_call | solution.py:693
  166.0 0.0 copy-start
  166.0 3.2 %copy.14 = bf16[512,2048]{1,0:T(8,128)(2,1)} copy(bf16[512,2048]{1,0:T(8,128)(2,1)} %get-tuple-element.4) | data formatting | bytes 4194304
  169.1 0.0 copy-done
  169.1 0.6 copy.15
Async XLA Ops:
  166.0 3.2 %copy-start = (bf16[4,256]{1,0:T(4,128)(2,1)S(1)}, bf16[4,256]{1,0:T(4,128)(2,1)}, u32[]{:S(2)}) copy-start(bf16[4,256]{1,0:T(4,128)(2,1)} %get-tuple-element.5) | copy-start | bytes 6148

commit v4 on v3

--- a/solution.py
+++ b/solution.py
@@ -506,6 +506,11 @@
         project(n - 1, 1 - core, True)
 
     begin(2)
+
+    @pl.loop(4, 7)
+    def _(e):
+        event(1, e)
+
     small_forward(1)
     project(15, 1 - core, True)
 
@@ -552,7 +557,7 @@
         weights = jnp.exp2((scores - peak) * scale2)
         weight_sum = jnp.sum(weights, axis=0, keepdims=True)
         summed = mxu(values, weights.astype(jnp.bfloat16))
-        return (summed / weight_sum).astype(jnp.bfloat16)
+        return (summed * (1.0 / weight_sum)).astype(jnp.bfloat16)
 
     def uk_uv(m, hh):
         base = hh * (DN + DV)
@@ -564,19 +569,13 @@
         )
         return w_uk, w_uv_t
 
-    @pl.loop(4, 15)
-    def _(e):
-        event(1, e)
-
-        @pl.when(e >= 11)
-        def _():
-            event(2, e - 11)
-
     @pl.loop(0, mp_size)
-    def _(m):
+    def _(k):
+        event(1, 7 + k)
+        m = z_at(lax.rem(k, z_size)) * 2 + lax.rem(y + k // z_size, 2)
         sibling_arrived(1, m)
         for hh in range(2):
-            event(2, 4 + 2 * m + hh)
+            event(2, 2 * k + hh)
             first = pl.multiple_of(m * 2 * (DN + DR), 2 * (DN + DR)) + hh * (DN + DR)
             first = pl.multiple_of(first, 64)
             w_uk, w_uv_t = uk_uv(m, hh)
@@ -613,8 +612,9 @@
         lax.broadcasted_iota(jnp.int32, (8, STEP_ROWS), 0), requests
     )
     bias = jnp.concatenate([bias, jnp.where(own, 0.0, MASKED)], axis=1)
-    bias = jnp.concatenate([bias] * (STEP_LANES // 8), axis=0)
-    scores = mxu(q_steps[...].T.astype(jnp.bfloat16), all_keys, NT) + bias
+    live = H * requests
+    bias = jnp.concatenate([bias] * (live // 8), axis=0)
+    scores = mxu(q_steps[...].T[:live].astype(jnp.bfloat16), all_keys, NT) + bias
     peak = jnp.max(scores, axis=1, keepdims=True)
     weights = jnp.exp2((scores - peak) * scale2)
     weight_sum = jnp.sum(weights, axis=1, keepdims=True)

time: 170 us -> 167 us (0.982)
  Pallas kernels: 165 us -> 162 us
    pallas_call x1, Pallas kernels: 165 us -> 162 us  [fused_device(): pl.pallas_call(functools.partial(fused_kernel, sizes), out_shape=(jax.Sha...]
where the time goes in v4:
time: 167 us
  Pallas kernels  162 us (97%)
  local copies, waits for them, and re-layouts  3.74 us (2%)
    pallas_call x1, Pallas kernels, fused_device(): pl.pallas_call(functools.partial(fused_kernel, sizes), out_shape=(jax.Sha...  162 us
    unnamed x4, local copies, waits for them, and re-layouts  3.74 us

profile of v4, /device:TPU:0, one launch (start us, length us, event | category | flops | bytes accessed | tf_op | source)
XLA Modules:
  0.0 166.6 jit_solution(15924327002808930006)
XLA Ops:
  0.6 162.2 %shard_map.113 = (bf16[512,2048]{1,0:T(8,128)(2,1)}, bf16[4,256]{1,0:T(4,128)(2,1)}) custom-call(bf16[512,2048]{1,0:T(8,128)(2,1)} %x_ref.1, bf16[4,256]{1,0:T(4,128)(2,1)} %step_ref.1, f32[1,2048]{1,0:T(1,128)} %bitcast.6, f32[1,512]{1,0:T(1,128)} %bitcast.7, f32[456,512]{1,0:T(8,128)} %bitcast.4, f32[128,512]{1,0:T(8,128)} %up_ref.1, ...), custom_call_target="tpu_custom_call" | custom-call | tf_op jit(solution)/shard_map/pallas_call | solution.py:693
  162.8 0.0 copy-start
  162.8 3.2 %copy.14 = bf16[512,2048]{1,0:T(8,128)(2,1)} copy(bf16[512,2048]{1,0:T(8,128)(2,1)} %get-tuple-element.4) | data formatting | bytes 4194304
  166.0 0.0 copy-done
  166.0 0.6 copy.15
Async XLA Ops:
  162.8 3.2 %copy-start = (bf16[4,256]{1,0:T(4,128)(2,1)S(1)}, bf16[4,256]{1,0:T(4,128)(2,1)}, u32[]{:S(2)}) copy-start(bf16[4,256]{1,0:T(4,128)(2,1)} %get-tuple-element.5) | copy-start | bytes 6148

commit v5 on v4

--- a/solution.py
+++ b/solution.py
@@ -493,21 +493,23 @@
     def _(n):
         event(0, n - 1)
 
-        @pl.when(n == 7)
+        @pl.when(n == 4)
         def _():
             begin(1)
             small_begin(1)
 
-        @pl.when(n >= 12)
-        def _():
-            event(1, n - 12)
+        @pl.when(n == 11)
+        def _():
+            begin(2)
+
+        @pl.when(n >= 10)
+        def _():
+            event(1, n - 10)
 
         project(n, core, False)
         project(n - 1, 1 - core, True)
 
-    begin(2)
-
-    @pl.loop(4, 7)
+    @pl.loop(6, 7)
     def _(e):
         event(1, e)
 

time: 167 us -> 169 us (1.012)
  Pallas kernels: 162 us -> 165 us
    pallas_call x1, Pallas kernels: 162 us -> 165 us  [fused_device(): pl.pallas_call(functools.partial(fused_kernel, sizes), out_shape=(jax.Sha...]
where the time goes in v5:
time: 169 us
  Pallas kernels  165 us (98%)
  local copies, waits for them, and re-layouts  3.74 us (2%)
    pallas_call x1, Pallas kernels, fused_device(): pl.pallas_call(functools.partial(fused_kernel, sizes), out_shape=(jax.Sha...  165 us
    unnamed x4, local copies, waits for them, and re-layouts  3.74 us

profile of v5, /device:TPU:0, one launch (start us, length us, event | category | flops | bytes accessed | tf_op | source)
XLA Modules:
  0.0 169.0 jit_solution(12786444916330689712)
XLA Ops:
  0.6 164.6 %shard_map.113 = (bf16[512,2048]{1,0:T(8,128)(2,1)}, bf16[4,256]{1,0:T(4,128)(2,1)}) custom-call(bf16[512,2048]{1,0:T(8,128)(2,1)} %x_ref.1, bf16[4,256]{1,0:T(4,128)(2,1)} %step_ref.1, f32[1,2048]{1,0:T(1,128)} %bitcast.6, f32[1,512]{1,0:T(1,128)} %bitcast.7, f32[456,512]{1,0:T(8,128)} %bitcast.4, f32[128,512]{1,0:T(8,128)} %up_ref.1, ...), custom_call_target="tpu_custom_call" | custom-call | tf_op jit(solution)/shard_map/pallas_call | solution.py:695
  165.2 0.0 copy-start
  165.2 3.2 %copy.14 = bf16[512,2048]{1,0:T(8,128)(2,1)} copy(bf16[512,2048]{1,0:T(8,128)(2,1)} %get-tuple-element.4) | data formatting | bytes 4194304
  168.4 0.0 copy-done
  168.4 0.6 copy.15
Async XLA Ops:
  165.2 3.2 %copy-start = (bf16[4,256]{1,0:T(4,128)(2,1)S(1)}, bf16[4,256]{1,0:T(4,128)(2,1)}, u32[]{:S(2)}) copy-start(bf16[4,256]{1,0:T(4,128)(2,1)} %get-tuple-element.5) | copy-start | bytes 6148
